TPU v7x, 768 devices: a whole 4x8x12 slice. The times are simulated.
768 devices in a mesh: section: 8 (over x, core), expert: 12 (over z), dp: 8 (over y).
Axes of the slice: x: 4, y: 8, z: 12, core: 2. Of those that a mesh axis runs over, the one named last changes fastest.
Arguments:
- out_grad: bfloat16 [8, 1536, 7168], P('section', ('expert', 'dp')), may hold values from -6 to 6
- expert_ids: int32 [8, 1536, 1], P('section', ('expert', 'dp')), may hold values from 0 to 11; in each aligned block of 16 rows (0 to 15, 16 to 31, ..., all dimensions but the last counted through in order) at most 2 rows name the same one
- gate_weight: float32 [8, 1536, 1], P('section', ('expert', 'dp')), may hold values from 0.1 to 1
- gate_pre: bfloat16 [8, 12, 192, 1024], P('section', 'expert'), may hold values from -6 to 6
- up_pre: bfloat16 [8, 12, 192, 1024], P('section', 'expert'), may hold values from -6 to 6
- w_gate: bfloat16 [12, 7168, 1024], P('expert', 'dp'), may hold values from -0.0625 to 0.0625
- w_up: bfloat16 [12, 7168, 1024], P('expert', 'dp'), may hold values from -0.0625 to 0.0625
- w_down: bfloat16 [12, 1024, 7168], P('expert', None, 'dp'), may hold values from -0.1875 to 0.1875
Outputs:
- handed: bfloat16 [8, 1536, 7168], P('section', ('expert', 'dp'))
- grad_down: bfloat16 [8, 12, 1024, 7168], P('section', 'expert', None, 'dp')
Inputs may be any that keep to these rules, and one draw needn't show every extreme that they name: `expert_ids`: each token names 1 expert. Among the 16 tokens of one device no expert is named more than 2 times, and in every draw some device's tokens name some expert exactly 2 times.
All inputs are finite; a program needn't handle non-finite values.
Results may differ from a plain program's by a relative error of at most 0.013.
Values may be sent and summed in bfloat16 or wider, within the bound.
No kernel may reach another device: no remote copies, remote signals or barrier semaphores. Data moves between devices by JAX's collectives and lax.ppermute only.
A program may use at most 32 MiB of HBM per device.

v0:
```python
import jax
import jax.numpy as jnp
from jax import lax
from jax.sharding import PartitionSpec as P


def shifted(value, axis, steps):
    count = lax.axis_size(axis)
    pairs = [(source, (source + steps) % count) for source in range(count)]
    return lax.ppermute(value, axis, pairs)


def slot_numbers(ids, count):
    flat = ids.reshape(-1)
    onehot = (flat[:, None] == jnp.arange(count, dtype=jnp.int32)[None, :]).astype(jnp.int32)
    before = jnp.cumsum(onehot, axis=0) - onehot
    return jnp.sum(before * onehot, axis=1).reshape(ids.shape)


def local_grads(partial_value, gvalue, uvalue):
    sigma = jax.nn.sigmoid(gvalue)
    gate_grad = (partial_value * uvalue * sigma * (1.0 + gvalue * (1.0 - sigma))).astype(
        jnp.bfloat16
    )
    up_grad = (partial_value * gvalue * sigma).astype(jnp.bfloat16)
    return (gate_grad, up_grad)


def on_device(out_grad, expert_ids, gate_weight, gate_pre, up_pre, w_gate, w_up, w_down):
    n_expert = lax.axis_size("expert")
    n_replica = lax.axis_size("dp")
    grad = out_grad[0]
    ids = expert_ids[0]
    tok_count = grad.shape[0]
    width = grad.shape[1]
    rows = gate_pre.shape[2]
    slots_per = rows // (n_replica * n_expert)
    target = ids * slots_per + slot_numbers(ids, n_expert)
    places = (
        target.reshape(-1)[None, :] == jnp.arange(n_expert * slots_per, dtype=jnp.int32)[:, None]
    )
    dispatch = jnp.sum(
        places.reshape(n_expert * slots_per, tok_count, -1).astype(jnp.float32), axis=2
    ).astype(jnp.bfloat16)
    send = jnp.dot(dispatch, grad, preferred_element_type=jnp.float32).astype(jnp.bfloat16)
    send = send.reshape(1, n_expert, slots_per, width)
    routed = lax.all_to_all(
        lax.all_to_all(send, "expert", split_axis=1, concat_axis=1, tiled=True),
        "dp",
        split_axis=3,
        concat_axis=0,
        tiled=True,
    )
    slab = routed.shape[3]
    routed = routed.reshape(rows, slab)
    weight_down = w_down[0]
    partial_value = lax.dot_general(
        routed, weight_down, (((1,), (1,)), ((), ())), preferred_element_type=jnp.float32
    )
    gvalue = gate_pre[0, 0].astype(jnp.float32)
    uvalue = up_pre[0, 0].astype(jnp.float32)
    hidden = (gvalue * jax.nn.sigmoid(gvalue) * uvalue).astype(jnp.bfloat16)
    down_grad = lax.dot_general(
        hidden, routed, (((0,), (0,)), ((), ())), preferred_element_type=jnp.float32
    )
    summed = lax.psum(partial_value.astype(jnp.bfloat16), "dp").astype(jnp.float32)
    gate_grad, up_grad = local_grads(summed, gvalue, uvalue)
    back = lax.dot_general(
        gate_grad, w_gate[0], (((1,), (1,)), ((), ())), preferred_element_type=jnp.float32
    )
    back = back + lax.dot_general(
        up_grad, w_up[0], (((1,), (1,)), ((), ())), preferred_element_type=jnp.float32
    )
    back = back.astype(jnp.bfloat16).reshape(n_replica, n_expert, slots_per, slab)
    returned = lax.all_to_all(
        lax.all_to_all(back, "expert", split_axis=1, concat_axis=1, tiled=True),
        "dp",
        split_axis=0,
        concat_axis=3,
        tiled=True,
    )
    flat = returned.reshape(n_expert * slots_per, width)
    picked = (
        jnp.take(flat, target.reshape(-1), axis=0).reshape(tok_count, -1, width).astype(jnp.float32)
    )
    total = grad.astype(jnp.float32) + jnp.sum(gate_weight[0][:, :, None] * picked, axis=1)
    handed = shifted(total.astype(jnp.bfloat16), "section", -1)
    return (handed[None], down_grad.astype(jnp.bfloat16)[None, None])


def solution(mesh):
    placed = (
        P("section", ("expert", "dp"), None),
        P("section", ("expert", "dp"), None),
        P("section", ("expert", "dp"), None),
        P("section", "expert", None, None),
        P("section", "expert", None, None),
        P("expert", "dp", None),
        P("expert", "dp", None),
        P("expert", None, "dp"),
    )
    return jax.shard_map(
        on_device,
        mesh=mesh,
        in_specs=placed,
        out_specs=(P("section", ("expert", "dp"), None), P("section", "expert", None, "dp")),
        check_vma=False,
    )
```

profile of v0, /device:TPU:1, one launch (start us, length us, event | category | flops | bytes accessed | tf_op | source)
XLA Modules:
  0.0 229.9 jit_solution(9075076147440178921)
XLA Ops:
  7.2 0.9 fusion.38
  8.1 0.8 select_reduce_fusion
  9.0 0.7 compare_and_fusion
  9.6 1.3 convolution_convert_fusion
  11.0 32.6 %all_to_all.40 = bf16[1,12,2,7168]{3,2,0,1:T(2,128)(2,1)S(1)} all-to-all(bf16[1,12,2,7168]{3,2,0,1:T(2,128)(2,1)S(1)} %bitcast.92), channel_id=1, replica_groups=mesh['section'=8,'expert'=12,'dp'=8] {'expert'}, dimensions={1} | all-to-all | bytes 688128 | tf_op jit(solution)/shard_map/all_to_all | solution.py:48
  43.7 6.1 %copy.21 = bf16[1,12,2,7168]{1,2,0,3:T(2,128)(2,1)} copy(bf16[1,12,2,7168]{3,2,0,1:T(2,128)(2,1)S(1)} %all_to_all.40) | data formatting | bytes 688128 | tf_op jit(solution)/shard_map/all_to_all | solution.py:48
  49.8 7.5 %reshape.161 = bf16[8,2,10752]{2,1,0:T(2,128)(2,1)S(1)} reshape(bf16[7168,1,2,12]{3,2,1,0:T(2,128)(2,1)} %bitcast.88) | data formatting | bytes 688128
  57.3 16.6 %all_to_all.41 = bf16[8,2,10752]{2,1,0:T(2,128)(2,1)S(1)} all-to-all(bf16[8,2,10752]{2,1,0:T(2,128)(2,1)S(1)} %reshape.161), channel_id=1, replica_groups=mesh['section'=8,'expert'=12,'dp'=8] {'dp'}, dimensions={0} | all-to-all | bytes 688128 | tf_op jit(solution)/shard_map/all_to_all | solution.py:47
  74.0 9.4 %reshape.162 = bf16[7168,1,2,12]{3,2,1,0:T(2,128)(2,1)} reshape(bf16[8,2,10752]{2,1,0:T(2,128)(2,1)S(1)} %all_to_all.41) | data formatting | bytes 688128
  83.4 5.7 %copy.27 = bf16[1,12,2,8,896]{4,3,2,1,0:T(8,128)(2,1)S(1)} copy(bf16[1,12,2,8,896]{1,2,4,3,0:T(2,128)(2,1)} %bitcast.89) | data formatting | bytes 688128 | tf_op jit(solution)/shard_map/all_to_all | solution.py:47
  89.1 0.3 copy.23
  89.5 1.5 fusion.9
  91.1 74.8 %all-reduce.2.cloned.1.call-done = bf16[192,1024]{1,0:T(8,128)(2,1)} async-done(((bf16[192,1024]{1,0:T(8,128)(2,1)}), bf16[192,1024]{1,0:T(8,128)(2,1)}) %all-reduce.2.cloned.1.call-update) | async-done | bytes 393232 | tf_op jit(solution)/shard_map/psum | solution.py:66
  165.9 2.6 %fusion = f32[192,896]{1,0:T(8,128)S(1)} fusion(bf16[1,896,1024]{2,1,0:T(8,128)(2,1)} %param.14, bf16[1,1,192,1024]{3,2,1,0:T(8,128)(2,1)S(1)} %copy-done.5, bf16[192,1024]{1,0:T(8,128)(2,1)} %all-reduce.2.cloned.1.call-done), kind=kOutput, calls=%fused_computation.2 | convolution fusion | flops 353894400 | bytes 3309568 | tf_op jit(solution)/shard_map/dot_general | solution.py:71
  168.6 0.9 fusion.12
  169.9 22.2 %all_to_all.42 = bf16[8,12,2,896]{3,2,0,1:T(2,128)(2,1)S(1)} all-to-all(bf16[8,12,2,896]{3,2,0,1:T(2,128)(2,1)S(1)} %copy.24), channel_id=1, replica_groups=mesh['section'=8,'expert'=12,'dp'=8] {'expert'}, dimensions={1} | all-to-all | bytes 688128 | tf_op jit(solution)/shard_map/all_to_all | solution.py:76
  192.1 1.0 copy.25
  193.1 4.4 %all-to-all-start.3 = ((bf16[8,12,2,896]{3,2,1,0:T(2,128)(2,1)}), bf16[8,12,2,896]{3,2,1,0:T(2,128)(2,1)S(1)}, u32[]{:S(2)}, u32[]{:S(2)}) async-start(bf16[8,12,2,896]{3,2,1,0:T(2,128)(2,1)} %copy.25), calls=%async_computation.3 | async-start | bytes 688128 | tf_op jit(solution)/shard_map/all_to_all | solution.py:75
  197.5 10.2 %all-to-all-done.3 = bf16[8,12,2,896]{3,2,1,0:T(2,128)(2,1)S(1)} async-done(((bf16[8,12,2,896]{3,2,1,0:T(2,128)(2,1)}), bf16[8,12,2,896]{3,2,1,0:T(2,128)(2,1)S(1)}, u32[]{:S(2)}, u32[]{:S(2)}) %all-to-all-start.3) | async-done | bytes 344096 | tf_op jit(solution)/shard_map/all_to_all | solution.py:75
  207.7 0.7 gather_fusion
  208.6 9.0 %collective-permute-start = (bf16[16,7168]{1,0:T(8,128)(2,1)S(1)}, bf16[16,7168]{1,0:T(8,128)(2,1)S(1)}, u32[]{:S(2)}, u32[]{:S(2)}) collective-permute-start(bf16[16,7168]{1,0:T(8,128)(2,1)S(1)} %add_convert_fusion), channel_id=1, source_target_pairs={{0,672},{96,0},{192,96},{288,192},{384,288},{480,384},{576,480},{6... | collective-permute-start | bytes 688136 | tf_op jit(solution)/shard_map/ppermute | solution.py:10
  217.6 3.0 %convert_bitcast_fusion = bf16[1,1,1024,896]{3,2,1,0:T(8,128)(2,1)} fusion(bf16[192,896]{1,0:T(8,128)(2,1)S(1)} %reshape.148, bf16[1,1,192,1024]{3,2,1,0:T(8,128)(2,1)} %param.12, bf16[1,1,192,1024]{3,2,1,0:T(8,128)(2,1)S(1)} %copy-done.5), kind=kOutput, calls=%fused_computation.8 | convolution fusion | flops 354811904 | bytes 2965504 | tf_op jit(solution)/shard_map/dot_general | solution.py:63
  220.6 1.8 collective-permute-done
  222.4 0.7 copy.31
  (28 shorter events, 1.0 us)
Async XLA Ops:
  7.2 82.4 %copy-start = (bf16[1,1024,896]{2,1,0:T(8,128)(2,1)S(1)}, bf16[1,1024,896]{2,1,0:T(8,128)(2,1)}, u32[]{:S(2)}) copy-start(bf16[1,1024,896]{2,1,0:T(8,128)(2,1)} %param.15) | copy-start | bytes 5505028
  7.2 158.8 %all-reduce.2.cloned.1.call-start = ((), (), s32[]{:S(2)}) async-start(), calls=%async_computation.4 | async-start | bytes 786432 | tf_op jit(solution)/shard_map/psum | solution.py:66
  89.4 76.6 %copy-start.5 = (bf16[1,1,192,1024]{3,2,1,0:T(8,128)(2,1)S(1)}, bf16[1,1,192,1024]{3,2,1,0:T(8,128)(2,1)}, u32[]{:S(2)}) copy-start(bf16[1,1,192,1024]{3,2,1,0:T(8,128)(2,1)} %param.11) | copy-start | bytes 1179652
  91.1 77.5 %copy-start.6 = (bf16[1,1,192,1024]{3,2,1,0:T(8,128)(2,1)S(1)}, bf16[1,1,192,1024]{3,2,1,0:T(8,128)(2,1)}, u32[]{:S(2)}) copy-start(bf16[1,1,192,1024]{3,2,1,0:T(8,128)(2,1)} %param.12) | copy-start | bytes 1179652
  165.9 2.6 %copy-start.4 = (bf16[1,896,1024]{2,1,0:T(8,128)(2,1)S(1)}, bf16[1,896,1024]{2,1,0:T(8,128)(2,1)}, u32[]{:S(2)}) copy-start(bf16[1,896,1024]{2,1,0:T(8,128)(2,1)} %param.13) | copy-start | bytes 5505028
  165.9 2.6 %copy-start.7 = (bf16[192,1024]{1,0:T(8,128)(2,1)S(1)}, bf16[192,1024]{1,0:T(8,128)(2,1)}, u32[]{:S(2)}) copy-start(bf16[192,1024]{1,0:T(8,128)(2,1)} %all-reduce.2.cloned.1.call-done) | copy-start | bytes 1179652
  169.5 27.9 %copy-start.2 = (s32[1,16,1]{1,2,0:T(1,128)S(1)}, s32[1,16,1]{1,2,0:T(1,128)}, u32[]{:S(2)}) copy-start(s32[1,16,1]{1,2,0:T(1,128)} %param.9) | copy-start | bytes 196
  193.1 14.6 %all-to-all-start.3 = ((bf16[8,12,2,896]{3,2,1,0:T(2,128)(2,1)}), bf16[8,12,2,896]{3,2,1,0:T(2,128)(2,1)S(1)}, u32[]{:S(2)}, u32[]{:S(2)}) async-start(bf16[8,12,2,896]{3,2,1,0:T(2,128)(2,1)} %copy.25), calls=%async_computation.3 | async-start | bytes 688128 | tf_op jit(solution)/shard_map/all_to_all | solution.py:75
  197.4 11.0 %copy-start.1 = (bf16[1,16,7168]{2,1,0:T(8,128)(2,1)S(1)}, bf16[1,16,7168]{2,1,0:T(8,128)(2,1)}, u32[]{:S(2)}) copy-start(bf16[1,16,7168]{2,1,0:T(8,128)(2,1)} %param.8) | copy-start | bytes 688132
  197.4 11.0 %copy-start.3 = (f32[1,16,1]{1,2,0:T(1,128)S(1)}, f32[1,16,1]{1,2,0:T(1,128)}, u32[]{:S(2)}) copy-start(f32[1,16,1]{1,2,0:T(1,128)} %param.10) | copy-start | bytes 196
  208.6 13.8 %collective-permute-start = (bf16[16,7168]{1,0:T(8,128)(2,1)S(1)}, bf16[16,7168]{1,0:T(8,128)(2,1)S(1)}, u32[]{:S(2)}, u32[]{:S(2)}) collective-permute-start(bf16[16,7168]{1,0:T(8,128)(2,1)S(1)} %add_convert_fusion), channel_id=1, source_target_pairs={{0,672},{96,0},{192,96},{288,192},{384,288},{480,384},{576,480},{6... | collective-permute-start | bytes 688136 | tf_op jit(solution)/shard_map/ppermute | solution.py:10
Sparse Core Ops, SparseCore 0:
  91.2 74.6 all-reduce.1
where the time goes:
time: 230 us
  waiting for transfers between devices  86.8 us (38%)
  blocking collectives  71.5 us (31%)
  local copies, waits for them, and re-layouts  32.1 us (14%)
  between operations  14.2 us (6%)
  starting transfers between devices  13.4 us (6%)
  matrix products  9.35 us (4%)
  other arithmetic  2.56 us (1%)
    psum x1, waiting for transfers between devices, on_device(): lax.psum(partial_value.astype(jnp.bfloat16), 'dp').astype(jnp.float32)  74.8 us
    all_to_all x1, blocking collectives, on_device(): lax.all_to_all(send, 'expert', split_axis=1, concat_axis=1, tiled=True)  32.6 us
    all_to_all x1, blocking collectives, on_device(): lax.all_to_all(back, 'expert', split_axis=1, concat_axis=1, tiled=True)  22.2 us
    unnamed x20, local copies, waits for them, and re-layouts  17.7 us
    all_to_all x1, blocking collectives, on_device(): lax.all_to_all(lax.all_to_all(send, 'expert', split_axis=1, concat_axis=1...  16.6 us
    all_to_all x1, waiting for transfers between devices, on_device(): lax.all_to_all(lax.all_to_all(back, 'expert', split_axis=1, concat_axis=1...  10.2 us
    ppermute x1, starting transfers between devices, shifted(): return lax.ppermute(value, axis, pairs)  8.97 us
    all_to_all x1, local copies, waits for them, and re-layouts, on_device(): lax.all_to_all(send, 'expert', split_axis=1, concat_axis=1, tiled=True)  6.12 us
  transfers between devices with their start and end apart: 3, of which 3 were waited for; matrix products, arithmetic and copies ran while one was open for 1% of the time, Pallas kernels for 0%

commit v1 on v0

v1 whole, which is shorter than its diff:
```python
import jax
import jax.numpy as jnp
from jax import lax
from jax.sharding import PartitionSpec as P


def shifted(value, axis, steps):
    count = lax.axis_size(axis)
    pairs = [(source, (source + steps) % count) for source in range(count)]
    return lax.ppermute(value, axis, pairs)


def exchange(value, axes):
    return lax.all_to_all(value, axes, split_axis=0, concat_axis=0, tiled=True)


def slot_numbers(ids, count):
    flat = ids.reshape(-1)
    onehot = (flat[:, None] == jnp.arange(count, dtype=jnp.int32)[None, :]).astype(jnp.int32)
    before = jnp.cumsum(onehot, axis=0) - onehot
    return jnp.sum(before * onehot, axis=1).reshape(ids.shape)


def on_device(out_grad, expert_ids, gate_weight, gate_pre, up_pre, w_gate, w_up, w_down):
    n_expert = lax.axis_size("expert")
    n_replica = lax.axis_size("dp")
    grad = out_grad[0]
    ids = expert_ids[0]
    tok_count = grad.shape[0]
    width = grad.shape[1]
    rows = gate_pre.shape[2]
    hidden_width = gate_pre.shape[3]
    slots_per = rows // (n_replica * n_expert)
    slab = width // n_replica
    n_slots = n_expert * slots_per
    target = ids * slots_per + slot_numbers(ids, n_expert)
    places = target.reshape(-1)[None, :] == jnp.arange(n_slots, dtype=jnp.int32)[:, None]
    dispatch = places.astype(jnp.bfloat16)
    send = jnp.dot(dispatch, grad, preferred_element_type=jnp.float32).astype(jnp.bfloat16)
    send = send.reshape(n_expert, slots_per, n_replica, slab).transpose(2, 0, 1, 3)
    send = send.reshape(n_replica * n_expert, slots_per, slab)
    routed = exchange(send, ("dp", "expert")).reshape(rows, slab)
    partial_value = lax.dot_general(
        routed, w_down[0], (((1,), (1,)), ((), ())), preferred_element_type=jnp.float32
    ).astype(jnp.bfloat16)
    per = rows // n_replica
    parts = exchange(partial_value.reshape(n_replica, per, hidden_width), "dp")
    own = jnp.sum(parts.astype(jnp.float32), axis=0).astype(jnp.bfloat16)
    spread = jnp.broadcast_to(own[None], (n_replica, per, hidden_width))
    summed = exchange(spread, "dp").reshape(rows, hidden_width).astype(jnp.float32)

    gvalue = gate_pre[0, 0].astype(jnp.float32)
    uvalue = up_pre[0, 0].astype(jnp.float32)
    sigma = jax.nn.sigmoid(gvalue)
    hidden = (gvalue * sigma * uvalue).astype(jnp.bfloat16)
    down_grad = lax.dot_general(
        hidden, routed, (((0,), (0,)), ((), ())), preferred_element_type=jnp.float32
    )
    gate_grad = (summed * uvalue * sigma * (1.0 + gvalue * (1.0 - sigma))).astype(jnp.bfloat16)
    up_grad = (summed * gvalue * sigma).astype(jnp.bfloat16)
    back = lax.dot_general(
        gate_grad, w_gate[0], (((1,), (1,)), ((), ())), preferred_element_type=jnp.float32
    )
    back = back + lax.dot_general(
        up_grad, w_up[0], (((1,), (1,)), ((), ())), preferred_element_type=jnp.float32
    )
    back = back.astype(jnp.bfloat16).reshape(n_replica * n_expert, slots_per, slab)
    returned = exchange(back, ("dp", "expert"))
    returned = returned.reshape(n_replica, n_slots, slab)
    picked = jnp.einsum(
        "st,dsf->tdf", dispatch, returned, preferred_element_type=jnp.float32
    ).reshape(tok_count, width)
    total = grad.astype(jnp.float32) + gate_weight[0] * picked
    handed = shifted(total.astype(jnp.bfloat16), "section", -1)
    return (handed[None], down_grad.astype(jnp.bfloat16)[None, None])


def solution(mesh):
    placed = (
        P("section", ("expert", "dp"), None),
        P("section", ("expert", "dp"), None),
        P("section", ("expert", "dp"), None),
        P("section", "expert", None, None),
        P("section", "expert", None, None),
        P("expert", "dp", None),
        P("expert", "dp", None),
        P("expert", None, "dp"),
    )
    return jax.shard_map(
        on_device,
        mesh=mesh,
        in_specs=placed,
        out_specs=(P("section", ("expert", "dp"), None), P("section", "expert", None, "dp")),
        check_vma=False,
    )
```

time: 230 us -> 117 us (0.51)
  waiting for transfers between devices: 86.8 us -> 1.79 us
  local copies, waits for them, and re-layouts: 32.1 us -> 2.36 us
  blocking collectives: 71.5 us -> 96 us
  between operations: 14.2 us -> 0.81 us
  starting transfers between devices: 13.4 us -> 6.02 us
  matrix products: 9.35 us -> 6.77 us
    psum x1 -> x0, waiting for transfers between devices: 74.8 us -> none  [on_device(): lax.psum(partial_value.astype(jnp.bfloat16), 'dp').astype(jnp.float32)]
    all_to_all x3 -> x4, blocking collectives: 71.5 us -> 96 us  [exchange(): return lax.all_to_all(value, axes, split_axis=0, concat_axis=0, tiled=True)]
    unnamed x20 -> x16, local copies, waits for them, and re-layouts: 17.7 us -> 1.64 us
    all_to_all x5 -> x0, local copies, waits for them, and re-layouts: 13.1 us -> none  [the longest x1 6.12 us: on_device(): lax.all_to_all(send, 'expert', split_axis=1, concat_axis=1, tiled=True)]
    all_to_all x1 -> x0, waiting for transfers between devices: 10.2 us -> none  [on_device(): lax.all_to_all(lax.all_to_all(back, 'expert', split_axis=1, concat_axis=1...]
    all_to_all x1 -> x0, starting transfers between devices: 4.36 us -> none  [on_device(): lax.all_to_all(lax.all_to_all(back, 'expert', split_axis=1, concat_axis=1...]
    ppermute x1, starting transfers between devices: 8.97 us -> 6.02 us  [shifted(): return lax.ppermute(value, axis, pairs)]
  transfers between devices with their start and end apart: 3 -> 1, of which waited for: 3 -> 1; matrix products, arithmetic and copies ran while one was open for 1% -> 3% of each run, Pallas kernels for 0% -> 0%
where the time goes in v1:
time: 117 us
  blocking collectives  96 us (82%)
  matrix products  6.77 us (6%)
  starting transfers between devices  6.02 us (5%)
  other arithmetic  3.06 us (3%)
  local copies, waits for them, and re-layouts  2.36 us (2%)
  waiting for transfers between devices  1.79 us (2%)
    all_to_all x4, blocking collectives, exchange(): return lax.all_to_all(value, axes, split_axis=0, concat_axis=0, tiled=True)  96 us
    ppermute x1, starting transfers between devices, shifted(): return lax.ppermute(value, axis, pairs)  6.02 us
    dot_general x1, matrix products, on_device(): lax.dot_general(hidden, routed, (((0,), (0,)), ((), ())), preferred_eleme...  3.01 us
  transfers between devices with their start and end apart: 1, of which 1 were waited for; matrix products, arithmetic and copies ran while one was open for 3% of the time, Pallas kernels for 0%

profile of v1, /device:TPU:1, one launch (start us, length us, event | category | flops | bytes accessed | tf_op | source)
XLA Modules:
  0.0 116.8 jit_solution(3437752727406763957)
XLA Ops:
  0.6 0.9 fusion.26
  1.5 0.8 select_reduce_fusion
  2.4 0.7 multiply_add_fusion
  3.0 1.2 convolution_convert_fusion
  4.3 0.3 copy.11
  4.5 40.1 %all_to_all.20 = bf16[96,2,896]{2,1,0:T(2,128)(2,1)S(1)} all-to-all(bf16[96,2,896]{2,1,0:T(2,128)(2,1)S(1)} %bitcast.54), channel_id=1, replica_groups=mesh['section'=8,'expert'=12,'dp'=8] {'dp','expert'}, dimensions={0} | all-to-all | bytes 688128 | tf_op jit(solution)/shard_map/all_to_all | solution.py:14
  44.7 0.1 reshape.54
  44.8 0.8 fusion.11
  45.6 16.0 %all_to_all.21 = bf16[8,24,1024]{2,1,0:T(8,128)(2,1)S(1)} all-to-all(bf16[8,24,1024]{2,1,0:T(8,128)(2,1)S(1)} %bitcast.50), channel_id=1, replica_groups=mesh['section'=8,'expert'=12,'dp'=8] {'dp'}, dimensions={0} | all-to-all | bytes 786432 | tf_op jit(solution)/shard_map/all_to_all | solution.py:14
  61.6 0.1 reduce_sum.22
  61.7 13.5 %all_to_all.22 = bf16[8,24,1024]{2,1,0:T(8,128)(2,1)S(1)} all-to-all(bf16[8,24,1024]{2,1,0:T(8,128)(2,1)S(1)} %broadcast_in_dim.6), channel_id=1, replica_groups=mesh['section'=8,'expert'=12,'dp'=8] {'dp'}, dimensions={0} | all-to-all | bytes 786432 | tf_op jit(solution)/shard_map/all_to_all | solution.py:14
  75.3 0.4 fusion.19
  75.7 0.2 fusion.21
  75.9 0.9 copy-done.2
  76.8 0.8 fusion.2
  77.6 0.8 fusion.14
  78.4 0.1 reshape.56
  78.5 26.2 %all_to_all.23 = bf16[96,2,896]{2,1,0:T(2,128)(2,1)S(1)} all-to-all(bf16[96,2,896]{2,1,0:T(2,128)(2,1)S(1)} %reshape.56), channel_id=1, replica_groups=mesh['section'=8,'expert'=12,'dp'=8] {'dp','expert'}, dimensions={0} | all-to-all | bytes 688128 | tf_op jit(solution)/shard_map/all_to_all | solution.py:14
  104.8 0.1 reshape.57
  105.0 0.3 fusion.1
  105.3 6.0 %collective-permute-start = (bf16[16,7168]{1,0:T(8,128)(2,1)S(1)}, bf16[16,7168]{1,0:T(8,128)(2,1)S(1)}, u32[]{:S(2)}, u32[]{:S(2)}) collective-permute-start(bf16[16,7168]{1,0:T(8,128)(2,1)S(1)} %fusion.1), channel_id=1, source_target_pairs={{0,672},{96,0},{192,96},{288,192},{384,288},{480,384},{576,480},{6... | collective-permute-start | bytes 688136 | tf_op jit(solution)/shard_map/ppermute | solution.py:10
  111.3 3.0 %convert_bitcast_fusion = bf16[1,1,1024,896]{3,2,1,0:T(8,128)(2,1)} fusion(bf16[192,896]{1,0:T(8,128)(2,1)S(1)} %reshape.54, bf16[1,1,192,1024]{3,2,1,0:T(8,128)(2,1)S(1)} %copy-done.4, bf16[1,1,192,1024]{3,2,1,0:T(8,128)(2,1)} %param.12), kind=kOutput, calls=%fused_computation.10 | convolution fusion | flops 354811904 | bytes 2965504 | tf_op jit(solution)/shard_map/dot_general | solution.py:56
  114.3 1.8 %collective-permute-done = bf16[16,7168]{1,0:T(8,128)(2,1)S(1)} collective-permute-done((bf16[16,7168]{1,0:T(8,128)(2,1)S(1)}, bf16[16,7168]{1,0:T(8,128)(2,1)S(1)}, u32[]{:S(2)}, u32[]{:S(2)}) %collective-permute-start) | collective-permute-done | bytes 229408 | tf_op jit(solution)/shard_map/ppermute | solution.py:10
  116.1 0.7 copy.16
  (17 shorter events, 0.2 us)
Async XLA Ops:
  0.6 44.2 %copy-start = (bf16[1,1024,896]{2,1,0:T(8,128)(2,1)S(1)}, bf16[1,1024,896]{2,1,0:T(8,128)(2,1)}, u32[]{:S(2)}) copy-start(bf16[1,1024,896]{2,1,0:T(8,128)(2,1)} %param.15) | copy-start | bytes 5505028
  45.6 29.7 %copy-start.4 = (bf16[1,1,192,1024]{3,2,1,0:T(8,128)(2,1)S(1)}, bf16[1,1,192,1024]{3,2,1,0:T(8,128)(2,1)}, u32[]{:S(2)}) copy-start(bf16[1,1,192,1024]{3,2,1,0:T(8,128)(2,1)} %param.11) | copy-start | bytes 1179652
  45.6 29.7 %copy-start.5 = (bf16[1,1,192,1024]{3,2,1,0:T(8,128)(2,1)S(1)}, bf16[1,1,192,1024]{3,2,1,0:T(8,128)(2,1)}, u32[]{:S(2)}) copy-start(bf16[1,1,192,1024]{3,2,1,0:T(8,128)(2,1)} %param.12) | copy-start | bytes 1179652
  75.3 1.5 %copy-start.2 = (bf16[1,896,1024]{2,1,0:T(8,128)(2,1)S(1)}, bf16[1,896,1024]{2,1,0:T(8,128)(2,1)}, u32[]{:S(2)}) copy-start(bf16[1,896,1024]{2,1,0:T(8,128)(2,1)} %param.14) | copy-start | bytes 5505028
  75.9 1.7 %copy-start.1 = (bf16[1,896,1024]{2,1,0:T(8,128)(2,1)S(1)}, bf16[1,896,1024]{2,1,0:T(8,128)(2,1)}, u32[]{:S(2)}) copy-start(bf16[1,896,1024]{2,1,0:T(8,128)(2,1)} %param.13) | copy-start | bytes 5505028
  78.4 26.6 %copy-start.3 = (bf16[1,16,7168]{2,1,0:T(8,128)(2,1)S(1)}, bf16[1,16,7168]{2,1,0:T(8,128)(2,1)}, u32[]{:S(2)}) copy-start(bf16[1,16,7168]{2,1,0:T(8,128)(2,1)} %param.8) | copy-start | bytes 688132
  78.4 26.6 %copy-start.6 = (f32[1,16,1]{1,2,0:T(1,128)S(1)}, f32[1,16,1]{1,2,0:T(1,128)}, u32[]{:S(2)}) copy-start(f32[1,16,1]{1,2,0:T(1,128)} %param.10) | copy-start | bytes 196
  105.3 10.8 %collective-permute-start = (bf16[16,7168]{1,0:T(8,128)(2,1)S(1)}, bf16[16,7168]{1,0:T(8,128)(2,1)S(1)}, u32[]{:S(2)}, u32[]{:S(2)}) collective-permute-start(bf16[16,7168]{1,0:T(8,128)(2,1)S(1)} %fusion.1), channel_id=1, source_target_pairs={{0,672},{96,0},{192,96},{288,192},{384,288},{480,384},{576,480},{6... | collective-permute-start | bytes 688136 | tf_op jit(solution)/shard_map/ppermute | solution.py:10

commit v2 on v1

v2 whole, which is shorter than its diff:
```python
import functools

import jax
import jax.numpy as jnp
from jax import lax
from jax.experimental import pallas as pl
from jax.experimental.pallas import tpu as pltpu
from jax.sharding import PartitionSpec as P

F32 = jnp.float32
BF16 = jnp.bfloat16


def shifted(value, axis, steps):
    count = lax.axis_size(axis)
    pairs = [(source, (source + steps) % count) for source in range(count)]
    return lax.ppermute(value, axis, pairs)


def exchange(value, axes):
    return lax.all_to_all(value, axes, split_axis=0, concat_axis=0, tiled=True)


def dispatch_kernel(slots_per, ids_ref, grad_ref, send_ref, places_ref):
    tokens = ids_ref.shape[1]
    slots = places_ref.shape[0]
    blocks, _, slab = send_ref.shape
    experts = slots // slots_per
    ids = ids_ref[...].astype(F32)
    across = jnp.broadcast_to(ids, (tokens, tokens))
    row = lax.broadcasted_iota(jnp.int32, (tokens, tokens), 0)
    col = lax.broadcasted_iota(jnp.int32, (tokens, tokens), 1)
    down = jnp.sum(jnp.where(row == col, across, 0.0), axis=1, keepdims=True)
    earlier = jnp.where((down == across) & (row < col), 1.0, 0.0)
    target = ids * slots_per + jnp.sum(earlier, axis=0, keepdims=True)
    slot = lax.broadcasted_iota(jnp.int32, (slots, tokens), 0).astype(F32)
    places = jnp.where(slot == target, 1.0, 0.0).astype(BF16)
    places_ref[...] = places
    for part in range(blocks // experts):
        piece = grad_ref[:, part * slab : (part + 1) * slab]
        moved = jnp.dot(places, piece, preferred_element_type=F32).astype(BF16)
        send_ref[part * experts : (part + 1) * experts] = moved.reshape(experts, slots_per, slab)


def add_kernel(parts_ref, out_ref):
    replicas = parts_ref.shape[0]
    total = parts_ref[0].astype(F32)
    for part in range(1, replicas):
        total = total + parts_ref[part].astype(F32)
    own = total.astype(BF16)
    for part in range(replicas):
        out_ref[part] = own


def back_kernel(h_ref, gate_ref, up_ref, wg_ref, wu_ref, out_ref, gate_grad, up_grad):
    rows, slab = gate_ref.shape[0], wg_ref.shape[0]
    blocks, slots_per, _ = out_ref.shape

    def chunk(index, carry):
        part = pl.ds(pl.multiple_of(index * 16, 16), 16)
        h = h_ref[part].astype(F32)
        g = gate_ref[part].astype(F32)
        u = up_ref[part].astype(F32)
        s = 1.0 / (1.0 + jnp.exp(-g))
        hs = h * s
        gate_grad[part] = (hs * u * (1.0 + g * (1.0 - s))).astype(BF16)
        up_grad[part] = (hs * g).astype(BF16)
        return carry

    lax.fori_loop(0, rows // 16, chunk, 0)
    dims = (((1,), (1,)), ((), ()))
    step = 256
    for start in range(0, slab, step):
        cols = slice(start, min(start + step, slab))
        value = lax.dot_general(gate_grad[...], wg_ref[cols, :], dims, preferred_element_type=F32)
        value = value + lax.dot_general(up_grad[...], wu_ref[cols, :], dims, preferred_element_type=F32)
        out_ref[:, :, cols] = value.astype(BF16).reshape(blocks, slots_per, cols.stop - cols.start)


def final_kernel(recv_ref, places_ref, weight_ref, grad_ref, out_ref):
    slots, tokens = places_ref.shape
    blocks, slots_per, slab = recv_ref.shape
    experts = slots // slots_per
    across = jnp.broadcast_to(weight_ref[...], (tokens, tokens))
    row = lax.broadcasted_iota(jnp.int32, (tokens, tokens), 0)
    col = lax.broadcasted_iota(jnp.int32, (tokens, tokens), 1)
    weight = jnp.sum(jnp.where(row == col, across, 0.0), axis=1, keepdims=True)
    dims = (((0,), (0,)), ((), ()))
    for part in range(blocks // experts):
        piece = recv_ref[part * experts : (part + 1) * experts].reshape(slots, slab)
        picked = lax.dot_general(places_ref[...], piece, dims, preferred_element_type=F32)
        cols = slice(part * slab, (part + 1) * slab)
        out_ref[:, cols] = (grad_ref[:, cols].astype(F32) + weight * picked).astype(BF16)


VM = pl.BlockSpec(memory_space=pltpu.VMEM)
ANY = pl.BlockSpec(memory_space=pl.ANY)


def limit(mebibytes):
    return pltpu.CompilerParams(vmem_limit_bytes=mebibytes << 20)


def on_device(out_grad, expert_ids, gate_weight, gate_pre, up_pre, w_gate, w_up, w_down):
    n_expert = lax.axis_size("expert")
    n_replica = lax.axis_size("dp")
    grad = out_grad[0]
    tok_count = grad.shape[0]
    width = grad.shape[1]
    rows = gate_pre.shape[2]
    hidden_width = gate_pre.shape[3]
    slots_per = rows // (n_replica * n_expert)
    slab = width // n_replica
    n_slots = n_expert * slots_per
    send, places = pl.pallas_call(
        functools.partial(dispatch_kernel, slots_per),
        out_shape=(
            jax.ShapeDtypeStruct((n_replica * n_expert, slots_per, slab), BF16),
            jax.ShapeDtypeStruct((n_slots, tok_count), BF16),
        ),
        in_specs=[VM, VM],
        out_specs=(VM, VM),
        compiler_params=limit(4),
        name="dispatch",
    )(expert_ids.reshape(1, tok_count), grad)
    routed = exchange(send, ("dp", "expert"))
    routed = routed.reshape(rows, slab)
    partial_value = lax.dot_general(
        routed, w_down[0], (((1,), (1,)), ((), ())), preferred_element_type=F32
    ).astype(BF16)
    per = rows // n_replica
    spread = jax.ShapeDtypeStruct((n_replica, per, hidden_width), BF16)
    partial_value = partial_value.reshape(n_replica, per, hidden_width)
    parts = exchange(partial_value, "dp")
    summed = pl.pallas_call(
        add_kernel,
        out_shape=spread,
        in_specs=[VM],
        out_specs=VM,
        compiler_params=limit(2),
        name="add",
    )(parts)
    summed = exchange(summed, "dp").reshape(rows, hidden_width)
    saved = pltpu.VMEM((rows, hidden_width), BF16)
    back = pl.pallas_call(
        back_kernel,
        out_shape=jax.ShapeDtypeStruct((n_replica * n_expert, slots_per, slab), BF16),
        in_specs=[VM] * 5,
        out_specs=VM,
        scratch_shapes=[saved, saved],
        compiler_params=limit(6),
        name="back",
    )(summed, gate_pre[0, 0], up_pre[0, 0], w_gate[0], w_up[0])
    returned = exchange(back, ("dp", "expert"))
    total = pl.pallas_call(
        final_kernel,
        out_shape=jax.ShapeDtypeStruct((tok_count, width), BF16),
        in_specs=[VM] * 4,
        out_specs=VM,
        compiler_params=limit(4),
        name="final",
    )(returned, places, gate_weight.reshape(1, tok_count), grad)
    handed = shifted(total, "section", -1)
    gvalue = gate_pre[0, 0].astype(F32)
    act = (gvalue * jax.nn.sigmoid(gvalue) * up_pre[0, 0].astype(F32)).astype(BF16)
    down_grad = lax.dot_general(act, routed, (((0,), (0,)), ((), ())), preferred_element_type=F32)
    return (handed[None], down_grad.astype(BF16)[None, None])


def solution(mesh):
    placed = (
        P("section", ("expert", "dp"), None),
        P("section", ("expert", "dp"), None),
        P("section", ("expert", "dp"), None),
        P("section", "expert", None, None),
        P("section", "expert", None, None),
        P("expert", "dp", None),
        P("expert", "dp", None),
        P("expert", None, "dp"),
    )
    return jax.shard_map(
        on_device,
        mesh=mesh,
        in_specs=placed,
        out_specs=(P("section", ("expert", "dp"), None), P("section", "expert", None, "dp")),
        check_vma=False,
    )
```

time: 117 us -> 114 us (0.974)
  matrix products: 6.77 us -> 2.79 us
  other arithmetic: 3.06 us -> 0 us
  Pallas kernels: 0 us -> 2.59 us
    dot_general x5 -> x1, matrix products: 6 us -> 2.01 us  [on_device(): lax.dot_general(act, routed, (((0,), (0,)), ((), ())), preferred_element_...]
    pallas_call x0 -> x4, Pallas kernels: none -> 2.59 us  [the longest x1 1.94 us: on_device(): pl.pallas_call(back_kernel, out_shape=jax.ShapeDtypeStruct((n_replica * n...]
    convert_element_type x3 -> x0, other arithmetic: 1.47 us -> none  [the longest x1 0.86 us: slot_numbers(): (flat[:, None] == jnp.arange(count, dtype=jnp.int32)[None, :]).astype(jnp...]
    unnamed x16 -> x19, local copies, waits for them, and re-layouts: 1.64 us -> 2.46 us
  transfers between devices with their start and end apart: 1 -> 1, of which waited for: 1 -> 1; matrix products, arithmetic and copies ran while one was open for 3% -> 2% of each run, Pallas kernels for 0% -> 0%
where the time goes in v2:
time: 114 us; the launch traced here: 113 us
  blocking collectives  96 us (84%)
  starting transfers between devices  6.02 us (5%)
  matrix products  2.79 us (2%)
  waiting for transfers between devices  2.78 us (2%)
  local copies, waits for them, and re-layouts  2.59 us (2%)
  Pallas kernels  2.59 us (2%)
    all_to_all x4, blocking collectives, exchange(): return lax.all_to_all(value, axes, split_axis=0, concat_axis=0, tiled=True)  96 us
    ppermute x1, starting transfers between devices, shifted(): return lax.ppermute(value, axis, pairs)  6.02 us
    ppermute x1, waiting for transfers between devices, shifted(): return lax.ppermute(value, axis, pairs)  2.78 us
    unnamed x19, local copies, waits for them, and re-layouts  2.46 us
  transfers between devices with their start and end apart: 1, of which 1 were waited for; matrix products, arithmetic and copies ran while one was open for 2% of the time, Pallas kernels for 0%

profile of v2, /device:TPU:1, one launch (start us, length us, event | category | flops | bytes accessed | tf_op | source)
XLA Modules:
  0.0 113.5 jit_solution(9483864548344901160)
XLA Ops:
  0.6 0.0 copy-start
  0.6 0.0 copy-start.3
  0.7 1.1 copy-done.3
  1.7 0.7 copy-done.7
  2.4 0.3 dispatch.1
  2.7 40.2 %all_to_all.20 = bf16[96,2,896]{2,1,0:T(2,128)(2,1)S(1)} all-to-all(bf16[96,2,896]{2,1,0:T(2,128)(2,1)S(1)} %get-tuple-element.4), channel_id=1, replica_groups=mesh['section'=8,'expert'=12,'dp'=8] {'dp','expert'}, dimensions={0} | all-to-all | bytes 688128 | tf_op jit(solution)/shard_map/all_to_all | solution.py:21
  42.9 0.1 reshape.21
  43.0 0.0 copy-start.1
  43.0 0.0 copy-start.2
  43.0 0.0 copy-start.5
  43.1 0.0 copy-start.6
  43.1 0.8 fusion.2
  43.9 16.0 %all_to_all.21.parts_ref = bf16[8,24,1024]{2,1,0:T(8,128)(2,1)S(1)} all-to-all(bf16[8,24,1024]{2,1,0:T(8,128)(2,1)S(1)} %bitcast.31), channel_id=1, replica_groups=mesh['section'=8,'expert'=12,'dp'=8] {'dp'}, dimensions={0} | all-to-all | bytes 786432 | tf_op jit(solution)/shard_map/all_to_all | solution.py:21
  59.8 0.1 add.18
  59.9 13.6 %all_to_all.22 = bf16[8,24,1024]{2,1,0:T(8,128)(2,1)S(1)} all-to-all(bf16[8,24,1024]{2,1,0:T(8,128)(2,1)S(1)} %add.18), channel_id=1, replica_groups=mesh['section'=8,'expert'=12,'dp'=8] {'dp'}, dimensions={0} | all-to-all | bytes 786432 | tf_op jit(solution)/shard_map/all_to_all | solution.py:21
  73.5 0.0 copy-start.4
  73.5 0.0 copy-start.8
  73.5 1.9 %back.1 = bf16[96,2,896]{2,1,0:T(2,128)(2,1)S(1)} custom-call(bf16[192,1024]{1,0:T(8,128)(2,1)S(1)} %bitcast.24, bf16[192,1024]{1,0:T(8,128)(2,1)S(1)} %bitcast.27, bf16[192,1024]{1,0:T(8,128)(2,1)S(1)} %bitcast.28, bf16[896,1024]{1,0:T(8,128)(2,1)S(1)} %bitcast.22, bf16[896,1024]{1,0:T(8,128)(2,1)S(1)} %bitcast.23), custom_call_target="tpu_custom_call" | custom-call | tf_op jit(solution)/shard_map/back/pallas_call | solution.py:145
  75.5 26.3 %all_to_all.23.recv_ref = bf16[96,2,896]{2,1,0:T(2,128)(2,1)S(1)} all-to-all(bf16[96,2,896]{2,1,0:T(2,128)(2,1)S(1)} %back.1), channel_id=1, replica_groups=mesh['section'=8,'expert'=12,'dp'=8] {'dp','expert'}, dimensions={0} | all-to-all | bytes 688128 | tf_op jit(solution)/shard_map/all_to_all | solution.py:21
  101.7 0.3 final.1
  102.0 6.0 %collective-permute-start = (bf16[16,7168]{1,0:T(8,128)(2,1)S(1)}, bf16[16,7168]{1,0:T(8,128)(2,1)S(1)}, u32[]{:S(2)}, u32[]{:S(2)}) collective-permute-start(bf16[16,7168]{1,0:T(8,128)(2,1)S(1)} %final.1), channel_id=1, source_target_pairs={{0,672},{96,0},{192,96},{288,192},{384,288},{480,384},{576,480},{6... | collective-permute-start | bytes 688136 | tf_op jit(solution)/shard_map/ppermute | solution.py:17
  108.0 2.0 %convert_bitcast_fusion = bf16[1,1,1024,896]{3,2,1,0:T(8,128)(2,1)} fusion(bf16[192,896]{1,0:T(8,128)(2,1)S(1)} %reshape.21, bf16[1,1,192,1024]{3,2,1,0:T(8,128)(2,1)S(1)} %copy-done.6, bf16[1,1,192,1024]{3,2,1,0:T(8,128)(2,1)S(1)} %copy-done.5), kind=kOutput, calls=%fused_computation.2 | convolution fusion | flops 354811904 | bytes 2965504 | tf_op jit(solution)/shard_map/dot_general | solution.py:166
  110.0 2.8 %collective-permute-done = bf16[16,7168]{1,0:T(8,128)(2,1)S(1)} collective-permute-done((bf16[16,7168]{1,0:T(8,128)(2,1)S(1)}, bf16[16,7168]{1,0:T(8,128)(2,1)S(1)}, u32[]{:S(2)}, u32[]{:S(2)}) %collective-permute-start) | collective-permute-done | bytes 229408 | tf_op jit(solution)/shard_map/ppermute | solution.py:17
  112.8 0.7 copy.11
  (8 shorter events, 0.0 us)
Async XLA Ops:
  0.6 42.4 %copy-start = (bf16[1,1024,896]{2,1,0:T(8,128)(2,1)S(1)}, bf16[1,1024,896]{2,1,0:T(8,128)(2,1)}, u32[]{:S(2)}) copy-start(bf16[1,1024,896]{2,1,0:T(8,128)(2,1)} %param.15) | copy-start | bytes 5505028
  0.6 1.1 copy-start.3
  1.7 0.7 copy-start.7
  43.0 30.4 %copy-start.1 = (bf16[1,896,1024]{2,1,0:T(8,128)(2,1)S(1)}, bf16[1,896,1024]{2,1,0:T(8,128)(2,1)}, u32[]{:S(2)}) copy-start(bf16[1,896,1024]{2,1,0:T(8,128)(2,1)} %param.13) | copy-start | bytes 5505028
  43.0 30.4 %copy-start.2 = (bf16[1,896,1024]{2,1,0:T(8,128)(2,1)S(1)}, bf16[1,896,1024]{2,1,0:T(8,128)(2,1)}, u32[]{:S(2)}) copy-start(bf16[1,896,1024]{2,1,0:T(8,128)(2,1)} %param.14) | copy-start | bytes 5505028
  43.0 30.4 %copy-start.5 = (bf16[1,1,192,1024]{3,2,1,0:T(8,128)(2,1)S(1)}, bf16[1,1,192,1024]{3,2,1,0:T(8,128)(2,1)}, u32[]{:S(2)}) copy-start(bf16[1,1,192,1024]{3,2,1,0:T(8,128)(2,1)} %param.11) | copy-start | bytes 1179652
  43.1 30.4 %copy-start.6 = (bf16[1,1,192,1024]{3,2,1,0:T(8,128)(2,1)S(1)}, bf16[1,1,192,1024]{3,2,1,0:T(8,128)(2,1)}, u32[]{:S(2)}) copy-start(bf16[1,1,192,1024]{3,2,1,0:T(8,128)(2,1)} %param.12) | copy-start | bytes 1179652
  73.5 28.2 %copy-start.4 = (bf16[1,16,7168]{2,1,0:T(8,128)(2,1)S(1)}, bf16[1,16,7168]{2,1,0:T(8,128)(2,1)}, u32[]{:S(2)}) copy-start(bf16[1,16,7168]{2,1,0:T(8,128)(2,1)} %param.8) | copy-start | bytes 688132
  73.5 28.2 %copy-start.8 = (f32[1,16,1]{1,2,0:T(1,128)S(1)}, f32[1,16,1]{1,2,0:T(1,128)}, u32[]{:S(2)}) copy-start(f32[1,16,1]{1,2,0:T(1,128)} %param.10) | copy-start | bytes 196
  102.0 10.8 %collective-permute-start = (bf16[16,7168]{1,0:T(8,128)(2,1)S(1)}, bf16[16,7168]{1,0:T(8,128)(2,1)S(1)}, u32[]{:S(2)}, u32[]{:S(2)}) collective-permute-start(bf16[16,7168]{1,0:T(8,128)(2,1)S(1)} %final.1), channel_id=1, source_target_pairs={{0,672},{96,0},{192,96},{288,192},{384,288},{480,384},{576,480},{6... | collective-permute-start | bytes 688136 | tf_op jit(solution)/shard_map/ppermute | solution.py:17

commit v3 on v2

--- a/solution.py
+++ b/solution.py
@@ -67,9 +67,9 @@
         up_grad[part] = (hs * g).astype(BF16)
         return carry
 
-    lax.fori_loop(0, rows // 16, chunk, 0)
+    lax.fori_loop(0, rows // 16, chunk, 0, unroll=True)
     dims = (((1,), (1,)), ((), ()))
-    step = 256
+    step = 896
     for start in range(0, slab, step):
         cols = slice(start, min(start + step, slab))
         value = lax.dot_general(gate_grad[...], wg_ref[cols, :], dims, preferred_element_type=F32)

time: 114 us -> 113 us (level)
  no operation moved by 1% of the time
where the time goes in v3:
time: 113 us
  blocking collectives  95.9 us (85%)
  starting transfers between devices  6.03 us (5%)
  matrix products  2.79 us (2%)
  waiting for transfers between devices  2.78 us (2%)
  local copies, waits for them, and re-layouts  2.59 us (2%)
  Pallas kernels  2.07 us (2%)
    all_to_all x4, blocking collectives, exchange(): return lax.all_to_all(value, axes, split_axis=0, concat_axis=0, tiled=True)  95.9 us
    ppermute x1, starting transfers between devices, shifted(): return lax.ppermute(value, axis, pairs)  6.03 us
    ppermute x1, waiting for transfers between devices, shifted(): return lax.ppermute(value, axis, pairs)  2.78 us
    unnamed x19, local copies, waits for them, and re-layouts  2.46 us
  transfers between devices with their start and end apart: 1, of which 1 were waited for; matrix products, arithmetic and copies ran while one was open for 2% of the time, Pallas kernels for 0%

profile of v3, /device:TPU:1, one launch (start us, length us, event | category | flops | bytes accessed | tf_op | source)
XLA Modules:
  0.0 113.0 jit_solution(15482492907295926692)
XLA Ops:
  0.6 0.0 copy-start
  0.6 0.0 copy-start.3
  0.7 1.1 copy-done.3
  1.7 0.7 copy-done.7
  2.4 0.3 dispatch.1
  2.7 40.2 %all_to_all.20 = bf16[96,2,896]{2,1,0:T(2,128)(2,1)S(1)} all-to-all(bf16[96,2,896]{2,1,0:T(2,128)(2,1)S(1)} %get-tuple-element.4), channel_id=1, replica_groups=mesh['section'=8,'expert'=12,'dp'=8] {'dp','expert'}, dimensions={0} | all-to-all | bytes 688128 | tf_op jit(solution)/shard_map/all_to_all | solution.py:21
  42.9 0.1 reshape.21
  43.0 0.0 copy-start.1
  43.0 0.0 copy-start.2
  43.0 0.0 copy-start.5
  43.1 0.0 copy-start.6
  43.1 0.8 fusion.2
  43.9 16.0 %all_to_all.21.parts_ref = bf16[8,24,1024]{2,1,0:T(8,128)(2,1)S(1)} all-to-all(bf16[8,24,1024]{2,1,0:T(8,128)(2,1)S(1)} %bitcast.31), channel_id=1, replica_groups=mesh['section'=8,'expert'=12,'dp'=8] {'dp'}, dimensions={0} | all-to-all | bytes 786432 | tf_op jit(solution)/shard_map/all_to_all | solution.py:21
  59.8 0.1 add.18
  59.9 13.6 %all_to_all.22 = bf16[8,24,1024]{2,1,0:T(8,128)(2,1)S(1)} all-to-all(bf16[8,24,1024]{2,1,0:T(8,128)(2,1)S(1)} %add.18), channel_id=1, replica_groups=mesh['section'=8,'expert'=12,'dp'=8] {'dp'}, dimensions={0} | all-to-all | bytes 786432 | tf_op jit(solution)/shard_map/all_to_all | solution.py:21
  73.5 0.0 copy-start.4
  73.5 0.0 copy-start.8
  73.5 1.4 %back.1 = bf16[96,2,896]{2,1,0:T(2,128)(2,1)S(1)} custom-call(bf16[192,1024]{1,0:T(8,128)(2,1)S(1)} %bitcast.24, bf16[192,1024]{1,0:T(8,128)(2,1)S(1)} %bitcast.27, bf16[192,1024]{1,0:T(8,128)(2,1)S(1)} %bitcast.28, bf16[896,1024]{1,0:T(8,128)(2,1)S(1)} %bitcast.22, bf16[896,1024]{1,0:T(8,128)(2,1)S(1)} %bitcast.23), custom_call_target="tpu_custom_call" | custom-call | tf_op jit(solution)/shard_map/back/pallas_call | solution.py:145
  74.9 26.2 %all_to_all.23.recv_ref = bf16[96,2,896]{2,1,0:T(2,128)(2,1)S(1)} all-to-all(bf16[96,2,896]{2,1,0:T(2,128)(2,1)S(1)} %back.1), channel_id=1, replica_groups=mesh['section'=8,'expert'=12,'dp'=8] {'dp','expert'}, dimensions={0} | all-to-all | bytes 688128 | tf_op jit(solution)/shard_map/all_to_all | solution.py:21
  101.2 0.3 final.1
  101.4 6.0 %collective-permute-start = (bf16[16,7168]{1,0:T(8,128)(2,1)S(1)}, bf16[16,7168]{1,0:T(8,128)(2,1)S(1)}, u32[]{:S(2)}, u32[]{:S(2)}) collective-permute-start(bf16[16,7168]{1,0:T(8,128)(2,1)S(1)} %final.1), channel_id=1, source_target_pairs={{0,672},{96,0},{192,96},{288,192},{384,288},{480,384},{576,480},{6... | collective-permute-start | bytes 688136 | tf_op jit(solution)/shard_map/ppermute | solution.py:17
  107.5 2.0 %convert_bitcast_fusion = bf16[1,1,1024,896]{3,2,1,0:T(8,128)(2,1)} fusion(bf16[192,896]{1,0:T(8,128)(2,1)S(1)} %reshape.21, bf16[1,1,192,1024]{3,2,1,0:T(8,128)(2,1)S(1)} %copy-done.6, bf16[1,1,192,1024]{3,2,1,0:T(8,128)(2,1)S(1)} %copy-done.5), kind=kOutput, calls=%fused_computation.2 | convolution fusion | flops 354811904 | bytes 2965504 | tf_op jit(solution)/shard_map/dot_general | solution.py:166
  109.5 2.8 %collective-permute-done = bf16[16,7168]{1,0:T(8,128)(2,1)S(1)} collective-permute-done((bf16[16,7168]{1,0:T(8,128)(2,1)S(1)}, bf16[16,7168]{1,0:T(8,128)(2,1)S(1)}, u32[]{:S(2)}, u32[]{:S(2)}) %collective-permute-start) | collective-permute-done | bytes 229408 | tf_op jit(solution)/shard_map/ppermute | solution.py:17
  112.3 0.7 copy.11
  (8 shorter events, 0.0 us)
Async XLA Ops:
  0.6 42.4 %copy-start = (bf16[1,1024,896]{2,1,0:T(8,128)(2,1)S(1)}, bf16[1,1024,896]{2,1,0:T(8,128)(2,1)}, u32[]{:S(2)}) copy-start(bf16[1,1024,896]{2,1,0:T(8,128)(2,1)} %param.15) | copy-start | bytes 5505028
  0.6 1.1 copy-start.3
  1.7 0.7 copy-start.7
  43.0 30.4 %copy-start.1 = (bf16[1,896,1024]{2,1,0:T(8,128)(2,1)S(1)}, bf16[1,896,1024]{2,1,0:T(8,128)(2,1)}, u32[]{:S(2)}) copy-start(bf16[1,896,1024]{2,1,0:T(8,128)(2,1)} %param.13) | copy-start | bytes 5505028
  43.0 30.4 %copy-start.2 = (bf16[1,896,1024]{2,1,0:T(8,128)(2,1)S(1)}, bf16[1,896,1024]{2,1,0:T(8,128)(2,1)}, u32[]{:S(2)}) copy-start(bf16[1,896,1024]{2,1,0:T(8,128)(2,1)} %param.14) | copy-start | bytes 5505028
  43.0 30.4 %copy-start.5 = (bf16[1,1,192,1024]{3,2,1,0:T(8,128)(2,1)S(1)}, bf16[1,1,192,1024]{3,2,1,0:T(8,128)(2,1)}, u32[]{:S(2)}) copy-start(bf16[1,1,192,1024]{3,2,1,0:T(8,128)(2,1)} %param.11) | copy-start | bytes 1179652
  43.1 30.4 %copy-start.6 = (bf16[1,1,192,1024]{3,2,1,0:T(8,128)(2,1)S(1)}, bf16[1,1,192,1024]{3,2,1,0:T(8,128)(2,1)}, u32[]{:S(2)}) copy-start(bf16[1,1,192,1024]{3,2,1,0:T(8,128)(2,1)} %param.12) | copy-start | bytes 1179652
  73.5 27.7 %copy-start.4 = (bf16[1,16,7168]{2,1,0:T(8,128)(2,1)S(1)}, bf16[1,16,7168]{2,1,0:T(8,128)(2,1)}, u32[]{:S(2)}) copy-start(bf16[1,16,7168]{2,1,0:T(8,128)(2,1)} %param.8) | copy-start | bytes 688132
  73.5 27.7 %copy-start.8 = (f32[1,16,1]{1,2,0:T(1,128)S(1)}, f32[1,16,1]{1,2,0:T(1,128)}, u32[]{:S(2)}) copy-start(f32[1,16,1]{1,2,0:T(1,128)} %param.10) | copy-start | bytes 196
  101.4 10.8 %collective-permute-start = (bf16[16,7168]{1,0:T(8,128)(2,1)S(1)}, bf16[16,7168]{1,0:T(8,128)(2,1)S(1)}, u32[]{:S(2)}, u32[]{:S(2)}) collective-permute-start(bf16[16,7168]{1,0:T(8,128)(2,1)S(1)} %final.1), channel_id=1, source_target_pairs={{0,672},{96,0},{192,96},{288,192},{384,288},{480,384},{576,480},{6... | collective-permute-start | bytes 688136 | tf_op jit(solution)/shard_map/ppermute | solution.py:17

commit v4 on v3

--- a/solution.py
+++ b/solution.py
@@ -15,6 +15,32 @@
     count = lax.axis_size(axis)
     pairs = [(source, (source + steps) % count) for source in range(count)]
     return lax.ppermute(value, axis, pairs)
+
+
+def turn_token():
+    sections, replicas = lax.axis_size("section"), lax.axis_size("dp")
+    pairs = [
+        (s * replicas + d, s * replicas + (d + 1) % replicas)
+        for s in range(0, sections, 2)
+        for d in range(replicas)
+    ]
+    return lax.ppermute(jnp.zeros((8, 128), F32), ("section", "dp"), pairs)
+
+
+def turn_kernel(value_ref, turn_ref, out_ref):
+    del value_ref, turn_ref, out_ref
+
+
+def in_turn(value, token):
+    return pl.pallas_call(
+        turn_kernel,
+        out_shape=jax.ShapeDtypeStruct(value.shape, value.dtype),
+        in_specs=[VM, VM],
+        out_specs=VM,
+        input_output_aliases={0: 0},
+        compiler_params=limit(2),
+        name="turn",
+    )(value, token)
 
 
 def exchange(value, axes):
@@ -123,6 +149,7 @@
         compiler_params=limit(4),
         name="dispatch",
     )(expert_ids.reshape(1, tok_count), grad)
+    send = in_turn(send, turn_token())
     routed = exchange(send, ("dp", "expert"))
     routed = routed.reshape(rows, slab)
     partial_value = lax.dot_general(

time: 113 us -> 109 us (0.965)
  blocking collectives: 95.9 us -> 87.4 us
  starting transfers between devices: 6.03 us -> 10.6 us
    all_to_all x4, blocking collectives: 95.9 us -> 87.4 us  [exchange(): return lax.all_to_all(value, axes, split_axis=0, concat_axis=0, tiled=True)]
    ppermute x1, starting transfers between devices: 6.03 us -> 9.77 us  [shifted(): return lax.ppermute(value, axis, pairs)]
  transfers between devices with their start and end apart: 1 -> 2, of which waited for: 1 -> 1; matrix products, arithmetic and copies ran while one was open for 2% -> 2% of each run, Pallas kernels for 0% -> 0%
where the time goes in v4:
time: 109 us
  blocking collectives  87.4 us (80%)
  starting transfers between devices  10.6 us (10%)
  matrix products  2.79 us (3%)
  waiting for transfers between devices  2.78 us (3%)
  local copies, waits for them, and re-layouts  2.46 us (2%)
  Pallas kernels  2.08 us (2%)
    all_to_all x4, blocking collectives, exchange(): return lax.all_to_all(value, axes, split_axis=0, concat_axis=0, tiled=True)  87.4 us
    ppermute x1, starting transfers between devices, shifted(): return lax.ppermute(value, axis, pairs)  9.77 us
    ppermute x1, waiting for transfers between devices, shifted(): return lax.ppermute(value, axis, pairs)  2.78 us
    unnamed x19, local copies, waits for them, and re-layouts  2.32 us
  transfers between devices with their start and end apart: 2, of which 1 were waited for; matrix products, arithmetic and copies ran while one was open for 2% of the time, Pallas kernels for 0%

profile of v4, /device:TPU:1, one launch (start us, length us, event | category | flops | bytes accessed | tf_op | source)
XLA Modules:
  0.0 108.8 jit_solution(1981780396860966158)
XLA Ops:
  0.6 0.0 copy-start
  0.7 0.8 collective-permute-start
  1.5 0.0 copy-start.3
  1.5 0.9 copy-done.3
  2.4 0.7 copy-done.7
  3.1 0.3 dispatch.1
  3.4 38.5 %all_to_all.20 = bf16[96,2,896]{2,1,0:T(2,128)(2,1)S(1)} all-to-all(bf16[96,2,896]{2,1,0:T(2,128)(2,1)S(1)} %turn.1), channel_id=1, replica_groups=mesh['section'=8,'expert'=12,'dp'=8] {'dp','expert'}, dimensions={0} | all-to-all | bytes 688128 | tf_op jit(solution)/shard_map/all_to_all | solution.py:47
  41.9 0.1 reshape.21
  42.1 0.0 copy-start.1
  42.1 0.0 copy-start.2
  42.1 0.0 copy-start.5
  42.1 0.0 copy-start.6
  42.1 0.8 fusion.2
  42.9 14.2 %all_to_all.21.parts_ref = bf16[8,24,1024]{2,1,0:T(8,128)(2,1)S(1)} all-to-all(bf16[8,24,1024]{2,1,0:T(8,128)(2,1)S(1)} %bitcast.31), channel_id=1, replica_groups=mesh['section'=8,'expert'=12,'dp'=8] {'dp'}, dimensions={0} | all-to-all | bytes 786432 | tf_op jit(solution)/shard_map/all_to_all | solution.py:47
  57.2 0.1 add.18
  57.2 13.1 %all_to_all.22 = bf16[8,24,1024]{2,1,0:T(8,128)(2,1)S(1)} all-to-all(bf16[8,24,1024]{2,1,0:T(8,128)(2,1)S(1)} %add.18), channel_id=1, replica_groups=mesh['section'=8,'expert'=12,'dp'=8] {'dp'}, dimensions={0} | all-to-all | bytes 786432 | tf_op jit(solution)/shard_map/all_to_all | solution.py:47
  70.4 0.0 copy-start.8
  70.4 1.4 %back.1 = bf16[96,2,896]{2,1,0:T(2,128)(2,1)S(1)} custom-call(bf16[192,1024]{1,0:T(8,128)(2,1)S(1)} %bitcast.24, bf16[192,1024]{1,0:T(8,128)(2,1)S(1)} %bitcast.27, bf16[192,1024]{1,0:T(8,128)(2,1)S(1)} %bitcast.28, bf16[896,1024]{1,0:T(8,128)(2,1)S(1)} %bitcast.22, bf16[896,1024]{1,0:T(8,128)(2,1)S(1)} %bitcast.23), custom_call_target="tpu_custom_call" | custom-call | tf_op jit(solution)/shard_map/back/pallas_call | solution.py:172
  71.8 21.5 %all_to_all.23.recv_ref = bf16[96,2,896]{2,1,0:T(2,128)(2,1)S(1)} all-to-all(bf16[96,2,896]{2,1,0:T(2,128)(2,1)S(1)} %back.1), channel_id=1, replica_groups=mesh['section'=8,'expert'=12,'dp'=8] {'dp','expert'}, dimensions={0} | all-to-all | bytes 688128 | tf_op jit(solution)/shard_map/all_to_all | solution.py:47
  93.3 0.3 final.1
  93.6 9.8 %collective-permute-start.1 = (bf16[16,7168]{1,0:T(8,128)(2,1)S(1)}, bf16[16,7168]{1,0:T(8,128)(2,1)S(1)}, u32[]{:S(2)}, u32[]{:S(2)}) collective-permute-start(bf16[16,7168]{1,0:T(8,128)(2,1)S(1)} %final.1), channel_id=1, source_target_pairs={{0,672},{96,0},{192,96},{288,192},{384,288},{480,384},{576,480},{6... | collective-permute-start | bytes 688136 | tf_op jit(solution)/shard_map/ppermute | solution.py:17
  103.4 2.0 %convert_bitcast_fusion = bf16[1,1,1024,896]{3,2,1,0:T(8,128)(2,1)} fusion(bf16[192,896]{1,0:T(8,128)(2,1)S(1)} %reshape.21, bf16[1,1,192,1024]{3,2,1,0:T(8,128)(2,1)S(1)} %copy-done.6, bf16[1,1,192,1024]{3,2,1,0:T(8,128)(2,1)S(1)} %copy-done.5), kind=kOutput, calls=%fused_computation.2 | convolution fusion | flops 354811904 | bytes 2965504 | tf_op jit(solution)/shard_map/dot_general | solution.py:193
  105.4 2.8 %collective-permute-done.1 = bf16[16,7168]{1,0:T(8,128)(2,1)S(1)} collective-permute-done((bf16[16,7168]{1,0:T(8,128)(2,1)S(1)}, bf16[16,7168]{1,0:T(8,128)(2,1)S(1)}, u32[]{:S(2)}, u32[]{:S(2)}) %collective-permute-start.1) | collective-permute-done | bytes 229408 | tf_op jit(solution)/shard_map/ppermute | solution.py:17
  108.2 0.7 copy.13
  (12 shorter events, 0.0 us)
Async XLA Ops:
  0.6 41.5 %copy-start = (bf16[1,1024,896]{2,1,0:T(8,128)(2,1)S(1)}, bf16[1,1024,896]{2,1,0:T(8,128)(2,1)}, u32[]{:S(2)}) copy-start(bf16[1,1024,896]{2,1,0:T(8,128)(2,1)} %param.15) | copy-start | bytes 5505028
  0.7 2.8 %collective-permute-start = (f32[8,128]{1,0:T(8,128)S(1)}, f32[8,128]{1,0:T(8,128)S(1)}, u32[]{:S(2)}, u32[]{:S(2)}) collective-permute-start(f32[8,128]{1,0:T(8,128)S(1)} %broadcast_in_dim.9), channel_id=1, source_target_pairs={{0,1},{1,2},{2,3},{3,4},{4,5},{5,6},{6,7},{7,0},{192,193},{193,194... | collective-permute-start | bytes 12296 | tf_op jit(solution)/shard_map/ppermute | solution.py:27
  1.5 0.9 copy-start.3
  2.4 0.7 copy-start.7
  42.1 28.3 %copy-start.1 = (bf16[1,896,1024]{2,1,0:T(8,128)(2,1)S(1)}, bf16[1,896,1024]{2,1,0:T(8,128)(2,1)}, u32[]{:S(2)}) copy-start(bf16[1,896,1024]{2,1,0:T(8,128)(2,1)} %param.13) | copy-start | bytes 5505028
  42.1 28.2 %copy-start.2 = (bf16[1,896,1024]{2,1,0:T(8,128)(2,1)S(1)}, bf16[1,896,1024]{2,1,0:T(8,128)(2,1)}, u32[]{:S(2)}) copy-start(bf16[1,896,1024]{2,1,0:T(8,128)(2,1)} %param.14) | copy-start | bytes 5505028
  42.1 28.2 %copy-start.5 = (bf16[1,1,192,1024]{3,2,1,0:T(8,128)(2,1)S(1)}, bf16[1,1,192,1024]{3,2,1,0:T(8,128)(2,1)}, u32[]{:S(2)}) copy-start(bf16[1,1,192,1024]{3,2,1,0:T(8,128)(2,1)} %param.11) | copy-start | bytes 1179652
  42.1 28.2 %copy-start.6 = (bf16[1,1,192,1024]{3,2,1,0:T(8,128)(2,1)S(1)}, bf16[1,1,192,1024]{3,2,1,0:T(8,128)(2,1)}, u32[]{:S(2)}) copy-start(bf16[1,1,192,1024]{3,2,1,0:T(8,128)(2,1)} %param.12) | copy-start | bytes 1179652
  70.4 23.0 %copy-start.4 = (bf16[1,16,7168]{2,1,0:T(8,128)(2,1)S(1)}, bf16[1,16,7168]{2,1,0:T(8,128)(2,1)}, u32[]{:S(2)}) copy-start(bf16[1,16,7168]{2,1,0:T(8,128)(2,1)} %param.8) | copy-start | bytes 688132
  70.4 22.9 %copy-start.8 = (f32[1,16,1]{1,2,0:T(1,128)S(1)}, f32[1,16,1]{1,2,0:T(1,128)}, u32[]{:S(2)}) copy-start(f32[1,16,1]{1,2,0:T(1,128)} %param.10) | copy-start | bytes 196
  93.6 14.6 %collective-permute-start.1 = (bf16[16,7168]{1,0:T(8,128)(2,1)S(1)}, bf16[16,7168]{1,0:T(8,128)(2,1)S(1)}, u32[]{:S(2)}, u32[]{:S(2)}) collective-permute-start(bf16[16,7168]{1,0:T(8,128)(2,1)S(1)} %final.1), channel_id=1, source_target_pairs={{0,672},{96,0},{192,96},{288,192},{384,288},{480,384},{576,480},{6... | collective-permute-start | bytes 688136 | tf_op jit(solution)/shard_map/ppermute | solution.py:17
